TPU v7x, 256 devices: a whole 4x4x8 slice. The times are simulated.
256 devices in a mesh: rep: 32 (over z_lo, y, core), fsdp: 8 (over z_hi, x).
Axes of the slice: x: 4, y: 4, z: 8 (z_hi: 2, z_lo: 4; z = z_hi * 4 + z_lo), core: 2. Of those that a mesh axis runs over, the one named last changes fastest.
Arguments:
- params: bfloat16 [32, 7168, 2048], P('rep', 'fsdp'), may hold values from -6 to 6
- hidden_acts: bfloat16 [32, 1024, 7168], P('rep', 'fsdp'), may hold values from -6 to 6
- out_grads: bfloat16 [32, 1024, 2048], P('rep', 'fsdp'), may hold values from -6 to 6
- step_counts: int32 [32], P('rep'), may hold values from 1 to 32
- outer_z: float32 [7168, 2048], P('fsdp', 'rep'), may hold values from -4 to 4
- outer_x: float32 [7168, 2048], P('fsdp', 'rep'), may hold values from -4 to 4
Outputs:
- new_z: float32 [7168, 2048], P('fsdp', 'rep')
- new_x: float32 [7168, 2048], P('fsdp', 'rep')
- new_y: bfloat16 [7168, 2048], P('fsdp')
All inputs are finite; a program needn't handle non-finite values.
Results may differ from a plain program's by a relative error of at most 0.0055.
Values may be sent and summed in bfloat16 or wider, within the bound.
A program may use at most 128 MiB of HBM per device.

v0:
```python
import jax
import jax.numpy as jnp
from jax import lax
from jax.sharding import Mesh
from jax.sharding import PartitionSpec as P

ROUND = 3
FSDP = ("fsdp_0", "fsdp_1")


def in_order(parts, dim):
    shape = list(parts.shape[1:])
    shape[dim] *= parts.shape[0]
    return jnp.moveaxis(parts, 0, dim).reshape(shape)


def all_blocks(array, axes, sequence):
    parts = array
    for k in sequence:
        parts = lax.all_gather(parts, axes[k])
    done = sequence[::-1]
    back = [done.index(k) for k in range(len(axes))]
    parts = parts.transpose(*back, *range(len(axes), parts.ndim))
    return parts.reshape(-1, *array.shape)


def gathered_by_axis(array, axes, sequence, dim):
    return in_order(all_blocks(array, axes, sequence), dim)


def sent_to_all(array, axis):
    copies = jnp.broadcast_to(array, (lax.axis_size(axis), *array.shape))
    return lax.all_to_all(copies, axis, split_axis=0, concat_axis=0, tiled=True)


def collect(array, axis, dim):
    parts = sent_to_all(array, axis)
    return in_order(parts, dim)


def transposed_product(left, right):
    return lax.dot_general(
        left, right, (((0,), (0,)), ((), ())), preferred_element_type=jnp.float32
    )


def local(params, hidden_acts, out_grads, step_counts, outer_z, outer_x):
    rows = params.shape[1]
    hidden_cols = lax.all_to_all(hidden_acts[0], FSDP, split_axis=1, concat_axis=0, tiled=True)
    grad = transposed_product(hidden_cols, gathered_by_axis(out_grads[0], FSDP, (0, 1), 0))
    inner = (params[0].astype(jnp.float32) - 0.1 * grad).astype(jnp.bfloat16)
    every_count = collect(step_counts, "rep", 0)
    replicas = every_count.shape[0]
    blocks = lax.all_to_all(inner, "rep", split_axis=1, concat_axis=0, tiled=True)
    columns = blocks.shape[1]
    stacked = blocks.reshape(replicas, rows * columns)
    weights = every_count.astype(jnp.bfloat16).reshape(1, replicas)
    summed = jnp.dot(weights, stacked, preferred_element_type=jnp.float32).reshape(rows, columns)
    total_f = jnp.sum(every_count).astype(jnp.float32)
    anchor = 0.1 * outer_z + 0.9 * outer_x
    pseudo = anchor - summed / total_f
    new_z = outer_z - 0.7 * pseudo
    mixing = 1.0 / (ROUND + 1.0)
    new_x = (1.0 - mixing) * outer_x + mixing * new_z
    block_y = (0.1 * new_z + 0.9 * new_x).astype(jnp.bfloat16)
    new_y = lax.all_gather(block_y, "rep", axis=1, tiled=True)
    return (new_z, new_x, new_y)


def solution(mesh):
    split = Mesh(mesh.devices.reshape(mesh.shape["rep"], 2, 4), ("rep", "fsdp_0", "fsdp_1"))
    placed = (
        P("rep", FSDP, None),
        P("rep", FSDP, None),
        P("rep", FSDP, None),
        P("rep"),
        P(FSDP, "rep"),
        P(FSDP, "rep"),
    )
    return jax.shard_map(
        local,
        mesh=split,
        in_specs=placed,
        out_specs=(P(FSDP, "rep"), P(FSDP, "rep"), P(FSDP, None)),
        check_vma=False,
    )
```

profile of v0, /device:TPU:1, one launch (start us, length us, event | category | flops | bytes accessed | tf_op | source)
XLA Modules:
  0.0 332.2 jit_solution(4786897905896339161)
XLA Ops:
  7.2 0.0 all-gather.5.cloned.1.call-start
  7.2 0.7 all-gather.5.cloned.1.call-update
  7.9 0.0 all-gather.9.cloned.1.call-start
  7.9 47.6 %all-gather.5.cloned.1.call-done = bf16[2,128,2048]{2,1,0:T(8,128)(2,1)} async-done(((bf16[1,128,2048]{2,1,0:T(8,128)(2,1)}), bf16[2,128,2048]{2,1,0:T(8,128)(2,1)}) %all-gather.5.cloned.1.call-update) | async-done | bytes 1048592 | tf_op jit(solution)/shard_map/all_gather | solution.py:20
  55.6 0.0 all-gather.9.cloned.1.call-update
  55.6 3.9 %copy.40 = bf16[1,128,7168]{1,2,0:T(8,128)(2,1)} copy(bf16[1,128,7168]{2,1,0:T(8,128)(2,1)} %param.7) | data formatting | bytes 3670016 | tf_op args[1]
  59.5 4.0 %all-to-all-start = ((bf16[128,8,896]{0,2,1:T(8,128)(2,1)}), bf16[128,8,896]{0,2,1:T(8,128)(2,1)S(1)}, u32[]{:S(2)}, u32[]{:S(2)}) async-start(bf16[128,8,896]{0,2,1:T(8,128)(2,1)} %bitcast.24), calls=%async_computation | async-start | bytes 3670016 | tf_op jit(solution)/shard_map/all_to_all | solution.py:49
  64.1 26.8 %all-to-all-done = bf16[128,8,896]{0,2,1:T(8,128)(2,1)S(1)} async-done(((bf16[128,8,896]{0,2,1:T(8,128)(2,1)}), bf16[128,8,896]{0,2,1:T(8,128)(2,1)S(1)}, u32[]{:S(2)}, u32[]{:S(2)}) %all-to-all-start) | async-done | bytes 1835040 | tf_op jit(solution)/shard_map/all_to_all | solution.py:49
  90.9 0.6 broadcast_in_dim.3
  91.5 25.4 %all-to-all-start.2 = ((s32[32,1,1]{2,1,0:T(1,128)}), s32[32,1,1]{2,1,0:T(1,128)S(1)}, u32[]{:S(2)}, u32[]{:S(2)}) async-start(s32[32,1,1]{2,1,0:T(1,128)} %broadcast_in_dim.3), calls=%async_computation.2 | async-start | bytes 32768 | tf_op jit(solution)/shard_map/all_to_all | solution.py:33
  116.9 2.6 copy.41
  119.5 1.8 all-gather.9.cloned.1.call-done
  121.3 0.0 copy-start
  121.3 0.0 copy-start.3
  121.3 2.7 copy.42
  123.9 0.1 copy-done
  124.0 1.1 copy-done.3
  125.1 5.7 %fusion = bf16[896,2048]{1,0:T(8,128)(2,1)} fusion(bf16[1024,896]{1,0:T(8,128)(2,1)S(1)} %bitcast.27, bf16[1024,2048]{1,0:T(8,128)(2,1)S(1)} %bitcast.26, bf16[1,896,2048]{2,1,0:T(8,128)(2,1)S(1)} %copy-done.3), kind=kOutput, calls=%fused_computation.2 | convolution fusion | flops 3765436416 | bytes 13369344 | tf_op jit(solution)/shard_map/dot_general | solution.py:42
  130.9 6.1 %copy.43 = bf16[896,2048]{0,1:T(8,128)(2,1)} copy(bf16[896,2048]{1,0:T(8,128)(2,1)} %fusion) | data formatting | bytes 7340032 | tf_op jit(solution)/shard_map/convert_element_type | solution.py:51
  136.9 0.0 all-to-all-done.2
  136.9 6.5 %all-to-all-start.1 = ((bf16[896,32,64]{0,2,1:T(8,128)(2,1)}), bf16[896,32,64]{0,2,1:T(8,128)(2,1)}, u32[]{:S(2)}, u32[]{:S(2)}) async-start(bf16[896,32,64]{0,2,1:T(8,128)(2,1)} %bitcast.21), calls=%async_computation.1 | async-start | bytes 7340032 | tf_op jit(solution)/shard_map/all_to_all | solution.py:54
  143.5 0.0 all-gather.7.cloned.1.call-start
  143.5 0.7 reduce_sum.9
  144.8 0.3 convert_reduce_fusion
  145.2 80.2 %all-to-all-done.1 = bf16[896,32,64]{0,2,1:T(8,128)(2,1)} async-done(((bf16[896,32,64]{0,2,1:T(8,128)(2,1)}), bf16[896,32,64]{0,2,1:T(8,128)(2,1)}, u32[]{:S(2)}, u32[]{:S(2)}) %all-to-all-start.1) | async-done | bytes 3670048 | tf_op jit(solution)/shard_map/all_to_all | solution.py:54
  225.4 7.8 %copy.44 = bf16[32,896,64]{2,1,0:T(8,128)(2,1)} copy(bf16[32,896,64]{1,2,0:T(8,128)(2,1)} %bitcast.9) | data formatting | bytes 7340032 | tf_op jit(solution)/shard_map/all_to_all | solution.py:54
  233.2 8.5 %reshape.37 = bf16[32,57344]{1,0:T(8,128)(2,1)} reshape(bf16[32,896,64]{2,1,0:T(8,128)(2,1)} %copy.44) | data formatting | bytes 7340032 | tf_op jit(solution)/shard_map/reshape | solution.py:56
  241.7 9.4 %dot_general.12 = bf16[896,64,32]{1,0,2:T(8,128)(2,1)} reshape(bf16[57344,32]{0,1:T(8,128)(2,1)} %bitcast.22) | data formatting | bytes 7340032 | tf_op jit(solution)/shard_map/dot_general | solution.py:58
  251.1 0.0 copy-start.1
  251.1 0.0 copy-start.2
  251.1 5.1 %multiply_reduce_fusion = f32[896,64]{1,0:T(8,128)S(1)} fusion(f32[32]{0:T(128)S(1)} %convert.2, bf16[896,64,32]{1,0,2:T(8,128)(2,1)} %dot_general.12), kind=kLoop, calls=%fused_computation | loop fusion | flops 5447680 | bytes 3899520
  256.2 0.2 copy.50
  256.4 0.0 copy-done.1
  256.4 0.0 copy-done.2
  256.4 0.9 add_convert_fusion
  257.3 0.0 all-gather.7.cloned.1.call-update
  257.3 62.3 %all-gather.7.cloned.1.call-done = bf16[896,2048]{0,1:T(8,128)(2,1)} async-done(((bf16[896,64]{0,1:T(8,128)(2,1)}), bf16[896,2048]{0,1:T(8,128)(2,1)}) %all-gather.7.cloned.1.call-update) | async-done | bytes 3670032 | tf_op jit(solution)/shard_map/all_gather | solution.py:66
  319.7 6.0 %copy.45 = bf16[896,2048]{1,0:T(8,128)(2,1)} copy(bf16[896,2048]{0,1:T(8,128)(2,1)} %all-gather.7.cloned.1.call-done) | data formatting | bytes 7340032
  (1 shorter events, 0.0 us)
Async XLA Ops:
  7.2 48.4 %all-gather.5.cloned.1.call-start = ((), (), s32[]{:S(2)}) async-start(), calls=%async_computation.3 | async-start | bytes 1572864 | tf_op jit(solution)/shard_map/all_gather | solution.py:20
  7.9 113.4 %all-gather.9.cloned.1.call-start = ((), (), s32[]{:S(2)}) async-start(), calls=%async_computation.5 | async-start | bytes 5242880 | tf_op jit(solution)/shard_map/all_gather | solution.py:20
  59.5 31.4 %all-to-all-start = ((bf16[128,8,896]{0,2,1:T(8,128)(2,1)}), bf16[128,8,896]{0,2,1:T(8,128)(2,1)S(1)}, u32[]{:S(2)}, u32[]{:S(2)}) async-start(bf16[128,8,896]{0,2,1:T(8,128)(2,1)} %bitcast.24), calls=%async_computation | async-start | bytes 3670016 | tf_op jit(solution)/shard_map/all_to_all | solution.py:49
  91.5 45.4 %all-to-all-start.2 = ((s32[32,1,1]{2,1,0:T(1,128)}), s32[32,1,1]{2,1,0:T(1,128)S(1)}, u32[]{:S(2)}, u32[]{:S(2)}) async-start(s32[32,1,1]{2,1,0:T(1,128)} %broadcast_in_dim.3), calls=%async_computation.2 | async-start | bytes 32768 | tf_op jit(solution)/shard_map/all_to_all | solution.py:33
  121.3 2.8 copy-start
  121.3 3.9 %copy-start.3 = (bf16[1,896,2048]{2,1,0:T(8,128)(2,1)S(1)}, bf16[1,896,2048]{2,1,0:T(8,128)(2,1)}, u32[]{:S(2)}) copy-start(bf16[1,896,2048]{2,1,0:T(8,128)(2,1)} %param.6) | copy-start | bytes 11010052
  136.9 88.5 %all-to-all-start.1 = ((bf16[896,32,64]{0,2,1:T(8,128)(2,1)}), bf16[896,32,64]{0,2,1:T(8,128)(2,1)}, u32[]{:S(2)}, u32[]{:S(2)}) async-start(bf16[896,32,64]{0,2,1:T(8,128)(2,1)} %bitcast.21), calls=%async_computation.1 | async-start | bytes 7340032 | tf_op jit(solution)/shard_map/all_to_all | solution.py:54
  143.5 176.2 %all-gather.7.cloned.1.call-start = ((), (), s32[]{:S(2)}) async-start(), calls=%async_computation.4 | async-start | bytes 3784704 | tf_op jit(solution)/shard_map/all_gather | solution.py:66
  251.1 5.3 %copy-start.1 = (f32[896,64]{0,1:T(8,128)S(1)}, f32[896,64]{0,1:T(8,128)}, u32[]{:S(2)}) copy-start(f32[896,64]{0,1:T(8,128)} %param.11) | copy-start | bytes 688132
  251.1 5.3 %copy-start.2 = (f32[896,64]{0,1:T(8,128)S(1)}, f32[896,64]{0,1:T(8,128)}, u32[]{:S(2)}) copy-start(f32[896,64]{0,1:T(8,128)} %param.10) | copy-start | bytes 688132
Sparse Core Ops, SparseCore 0:
  9.8 45.7 all-gather.4
  57.4 63.8 all-gather.8
  257.4 62.1 all-gather.6
where the time goes:
time: 333 us; the launch traced here: 332 us
  waiting for transfers between devices  219 us (66%)
  local copies, waits for them, and re-layouts  48.9 us (15%)
  starting transfers between devices  36 us (11%)
  between operations  15.1 us (5%)
  other arithmetic  7.03 us (2%)
  matrix products  5.74 us (2%)
    all_to_all x1, waiting for transfers between devices, local(): lax.all_to_all(inner, 'rep', split_axis=1, concat_axis=0, tiled=True)  80.2 us
    all_gather x1, waiting for transfers between devices, local(): new_y = lax.all_gather(block_y, 'rep', axis=1, tiled=True)  62.3 us
    all_gather x2, waiting for transfers between devices, all_blocks(): parts = lax.all_gather(parts, axes[k])  49.4 us
    all_to_all x1, waiting for transfers between devices, local(): lax.all_to_all(hidden_acts[0], FSDP, split_axis=1, concat_axis=0, tiled=T...  26.8 us
    all_to_all x1, starting transfers between devices, sent_to_all(): return lax.all_to_all(copies, axis, split_axis=0, concat_axis=0, tiled=True)  25.4 us
    unnamed x10, local copies, waits for them, and re-layouts  11.1 us
    dot_general x2, local copies, waits for them, and re-layouts, local(): jnp.dot(weights, stacked, preferred_element_type=jnp.float32)  9.55 us
    reshape x1, local copies, waits for them, and re-layouts, local(): stacked = blocks.reshape(replicas, rows * columns)  8.46 us
  transfers between devices with their start and end apart: 6, of which 5 were waited for; matrix products, arithmetic and copies ran while one was open for 7% of the time, Pallas kernels for 0%

commit v1 on v0

--- a/solution.py
+++ b/solution.py
@@ -63,7 +63,9 @@
     mixing = 1.0 / (ROUND + 1.0)
     new_x = (1.0 - mixing) * outer_x + mixing * new_z
     block_y = (0.1 * new_z + 0.9 * new_x).astype(jnp.bfloat16)
-    new_y = lax.all_gather(block_y, "rep", axis=1, tiled=True)
+    new_y = jnp.concatenate(
+        lax.all_to_all(jnp.stack([block_y] * lax.axis_size("rep")), "rep", 0, 0), axis=1
+    )
     return (new_z, new_x, new_y)
 
 

time: 333 us -> 362 us (1.087)
  blocking collectives: 0 us -> 90.3 us
  waiting for transfers between devices: 219 us -> 157 us
    all_to_all x0 -> x1, blocking collectives: none -> 90.3 us  [local(): lax.all_to_all(jnp.stack([block_y] * lax.axis_size('rep')), 'rep', 0, 0)]
    all_gather x1 -> x0, waiting for transfers between devices: 62.3 us -> none  [local(): new_y = lax.all_gather(block_y, 'rep', axis=1, tiled=True)]
  transfers between devices with their start and end apart: 6 -> 5, of which waited for: 5 -> 4; matrix products, arithmetic and copies ran while one was open for 7% -> 6% of each run, Pallas kernels for 0% -> 0%
where the time goes in v1:
time: 362 us; the launch traced here: 361 us
  waiting for transfers between devices  157 us (43%)
  blocking collectives  90.3 us (25%)
  local copies, waits for them, and re-layouts  49.5 us (14%)
  starting transfers between devices  35.9 us (10%)
  between operations  15.4 us (4%)
  other arithmetic  7.02 us (2%)
  matrix products  5.74 us (2%)
    all_to_all x1, blocking collectives, local(): lax.all_to_all(jnp.stack([block_y] * lax.axis_size('rep')), 'rep', 0, 0)  90.3 us
    all_to_all x1, waiting for transfers between devices, local(): lax.all_to_all(inner, 'rep', split_axis=1, concat_axis=0, tiled=True)  80.3 us
    all_gather x2, waiting for transfers between devices, all_blocks(): parts = lax.all_gather(parts, axes[k])  49.4 us
    all_to_all x1, waiting for transfers between devices, local(): lax.all_to_all(hidden_acts[0], FSDP, split_axis=1, concat_axis=0, tiled=T...  26.8 us
    all_to_all x1, starting transfers between devices, sent_to_all(): return lax.all_to_all(copies, axis, split_axis=0, concat_axis=0, tiled=True)  25.4 us
    unnamed x10, local copies, waits for them, and re-layouts  11.1 us
    dot_general x2, local copies, waits for them, and re-layouts, local(): jnp.dot(weights, stacked, preferred_element_type=jnp.float32)  9.57 us
    reshape x1, local copies, waits for them, and re-layouts, local(): stacked = blocks.reshape(replicas, rows * columns)  8.46 us
  transfers between devices with their start and end apart: 5, of which 4 were waited for; matrix products, arithmetic and copies ran while one was open for 6% of the time, Pallas kernels for 0%

profile of v1, /device:TPU:1, one launch (start us, length us, event | category | flops | bytes accessed | tf_op | source)
XLA Modules:
  0.0 361.0 jit_solution(7514978546248207988)
XLA Ops:
  7.2 0.0 all-gather.4.cloned.1.call-start
  7.2 0.7 all-gather.4.cloned.1.call-update
  7.9 0.0 all-gather.6.cloned.1.call-start
  7.9 47.6 %all-gather.4.cloned.1.call-done = bf16[2,128,2048]{2,1,0:T(8,128)(2,1)} async-done(((bf16[1,128,2048]{2,1,0:T(8,128)(2,1)}), bf16[2,128,2048]{2,1,0:T(8,128)(2,1)}) %all-gather.4.cloned.1.call-update) | async-done | bytes 1048592 | tf_op jit(solution)/shard_map/all_gather | solution.py:20
  55.6 0.0 all-gather.6.cloned.1.call-update
  55.6 3.9 %copy.25 = bf16[1,128,7168]{1,2,0:T(8,128)(2,1)} copy(bf16[1,128,7168]{2,1,0:T(8,128)(2,1)} %param.7) | data formatting | bytes 3670016 | tf_op args[1]
  59.5 4.0 %all-to-all-start = ((bf16[128,8,896]{0,2,1:T(8,128)(2,1)}), bf16[128,8,896]{0,2,1:T(8,128)(2,1)S(1)}, u32[]{:S(2)}, u32[]{:S(2)}) async-start(bf16[128,8,896]{0,2,1:T(8,128)(2,1)} %bitcast.28), calls=%async_computation | async-start | bytes 3670016 | tf_op jit(solution)/shard_map/all_to_all | solution.py:49
  64.1 26.8 %all-to-all-done = bf16[128,8,896]{0,2,1:T(8,128)(2,1)S(1)} async-done(((bf16[128,8,896]{0,2,1:T(8,128)(2,1)}), bf16[128,8,896]{0,2,1:T(8,128)(2,1)S(1)}, u32[]{:S(2)}, u32[]{:S(2)}) %all-to-all-start) | async-done | bytes 1835040 | tf_op jit(solution)/shard_map/all_to_all | solution.py:49
  90.9 0.6 broadcast_in_dim.3
  91.5 25.4 %all-to-all-start.2 = ((s32[32,1,1]{2,1,0:T(1,128)}), s32[32,1,1]{2,1,0:T(1,128)S(1)}, u32[]{:S(2)}, u32[]{:S(2)}) async-start(s32[32,1,1]{2,1,0:T(1,128)} %broadcast_in_dim.3), calls=%async_computation.2 | async-start | bytes 32768 | tf_op jit(solution)/shard_map/all_to_all | solution.py:33
  116.9 2.6 copy.26
  119.5 1.8 all-gather.6.cloned.1.call-done
  121.3 0.0 copy-start
  121.3 0.0 copy-start.3
  121.3 2.7 copy.27
  123.9 0.1 copy-done
  124.0 1.1 copy-done.3
  125.1 5.7 %fusion = bf16[896,2048]{1,0:T(8,128)(2,1)} fusion(bf16[1024,896]{1,0:T(8,128)(2,1)S(1)} %bitcast.31, bf16[1024,2048]{1,0:T(8,128)(2,1)S(1)} %bitcast.30, bf16[1,896,2048]{2,1,0:T(8,128)(2,1)S(1)} %copy-done.3), kind=kOutput, calls=%fused_computation.2 | convolution fusion | flops 3765436416 | bytes 13369344 | tf_op jit(solution)/shard_map/dot_general | solution.py:42
  130.9 6.1 %copy.28 = bf16[896,2048]{0,1:T(8,128)(2,1)} copy(bf16[896,2048]{1,0:T(8,128)(2,1)} %fusion) | data formatting | bytes 7340032 | tf_op jit(solution)/shard_map/convert_element_type | solution.py:51
  136.9 0.0 all-to-all-done.2
  136.9 6.5 %all-to-all-start.1 = ((bf16[896,32,64]{0,2,1:T(8,128)(2,1)}), bf16[896,32,64]{0,2,1:T(8,128)(2,1)}, u32[]{:S(2)}, u32[]{:S(2)}) async-start(bf16[896,32,64]{0,2,1:T(8,128)(2,1)} %bitcast.24), calls=%async_computation.1 | async-start | bytes 7340032 | tf_op jit(solution)/shard_map/all_to_all | solution.py:54
  143.5 0.7 reduce_sum.9
  144.8 0.3 convert_reduce_fusion
  145.1 80.3 %all-to-all-done.1 = bf16[896,32,64]{0,2,1:T(8,128)(2,1)} async-done(((bf16[896,32,64]{0,2,1:T(8,128)(2,1)}), bf16[896,32,64]{0,2,1:T(8,128)(2,1)}, u32[]{:S(2)}, u32[]{:S(2)}) %all-to-all-start.1) | async-done | bytes 3670048 | tf_op jit(solution)/shard_map/all_to_all | solution.py:54
  225.4 7.8 %copy.29 = bf16[32,896,64]{2,1,0:T(8,128)(2,1)} copy(bf16[32,896,64]{1,2,0:T(8,128)(2,1)} %bitcast.9) | data formatting | bytes 7340032 | tf_op jit(solution)/shard_map/all_to_all | solution.py:54
  233.2 8.5 %reshape.45 = bf16[32,57344]{1,0:T(8,128)(2,1)} reshape(bf16[32,896,64]{2,1,0:T(8,128)(2,1)} %copy.29) | data formatting | bytes 7340032 | tf_op jit(solution)/shard_map/reshape | solution.py:56
  241.7 9.4 %dot_general.12 = bf16[896,64,32]{1,0,2:T(8,128)(2,1)} reshape(bf16[57344,32]{0,1:T(8,128)(2,1)} %bitcast.26) | data formatting | bytes 7340032 | tf_op jit(solution)/shard_map/dot_general | solution.py:58
  251.1 0.0 copy-start.1
  251.1 0.0 copy-start.2
  251.1 5.1 %multiply_reduce_fusion = f32[896,64]{1,0:T(8,128)S(1)} fusion(f32[32]{0:T(128)S(1)} %convert.2, bf16[896,64,32]{1,0,2:T(8,128)(2,1)} %dot_general.12), kind=kLoop, calls=%fused_computation | loop fusion | flops 5447680 | bytes 3899520
  256.3 0.2 copy.35
  256.4 0.0 copy-done.1
  256.4 0.0 copy-done.2
  256.4 0.9 add_convert_fusion
  257.3 0.5 stack.2
  257.8 90.3 %all_to_all.46 = bf16[32,896,64]{1,2,0:T(8,128)(2,1)} all-to-all(bf16[32,896,64]{1,2,0:T(8,128)(2,1)S(1)} %stack.2), channel_id=1, replica_groups=mesh['rep'=32,'fsdp_0'=2,'fsdp_1'=4] {'rep'}, dimensions={0} | all-to-all | bytes 7340032 | tf_op jit(solution)/shard_map/all_to_all | solution.py:67
  348.1 6.0 %copy.30 = bf16[896,2048]{1,0:T(8,128)(2,1)} copy(bf16[896,2048]{0,1:T(8,128)(2,1)} %bitcast.25) | data formatting | bytes 7340032
  (1 shorter events, 0.0 us)
Async XLA Ops:
  7.2 48.4 %all-gather.4.cloned.1.call-start = ((), (), s32[]{:S(2)}) async-start(), calls=%async_computation.4 | async-start | bytes 1572864 | tf_op jit(solution)/shard_map/all_gather | solution.py:20
  7.9 113.4 %all-gather.6.cloned.1.call-start = ((), (), s32[]{:S(2)}) async-start(), calls=%async_computation.5 | async-start | bytes 5242880 | tf_op jit(solution)/shard_map/all_gather | solution.py:20
  59.5 31.4 %all-to-all-start = ((bf16[128,8,896]{0,2,1:T(8,128)(2,1)}), bf16[128,8,896]{0,2,1:T(8,128)(2,1)S(1)}, u32[]{:S(2)}, u32[]{:S(2)}) async-start(bf16[128,8,896]{0,2,1:T(8,128)(2,1)} %bitcast.28), calls=%async_computation | async-start | bytes 3670016 | tf_op jit(solution)/shard_map/all_to_all | solution.py:49
  91.5 45.4 %all-to-all-start.2 = ((s32[32,1,1]{2,1,0:T(1,128)}), s32[32,1,1]{2,1,0:T(1,128)S(1)}, u32[]{:S(2)}, u32[]{:S(2)}) async-start(s32[32,1,1]{2,1,0:T(1,128)} %broadcast_in_dim.3), calls=%async_computation.2 | async-start | bytes 32768 | tf_op jit(solution)/shard_map/all_to_all | solution.py:33
  121.3 2.8 copy-start
  121.3 3.9 %copy-start.3 = (bf16[1,896,2048]{2,1,0:T(8,128)(2,1)S(1)}, bf16[1,896,2048]{2,1,0:T(8,128)(2,1)}, u32[]{:S(2)}) copy-start(bf16[1,896,2048]{2,1,0:T(8,128)(2,1)} %param.6) | copy-start | bytes 11010052
  136.9 88.5 %all-to-all-start.1 = ((bf16[896,32,64]{0,2,1:T(8,128)(2,1)}), bf16[896,32,64]{0,2,1:T(8,128)(2,1)}, u32[]{:S(2)}, u32[]{:S(2)}) async-start(bf16[896,32,64]{0,2,1:T(8,128)(2,1)} %bitcast.24), calls=%async_computation.1 | async-start | bytes 7340032 | tf_op jit(solution)/shard_map/all_to_all | solution.py:54
  251.1 5.3 %copy-start.1 = (f32[896,64]{0,1:T(8,128)S(1)}, f32[896,64]{0,1:T(8,128)}, u32[]{:S(2)}) copy-start(f32[896,64]{0,1:T(8,128)} %param.11) | copy-start | bytes 688132
  251.1 5.3 %copy-start.2 = (f32[896,64]{0,1:T(8,128)S(1)}, f32[896,64]{0,1:T(8,128)}, u32[]{:S(2)}) copy-start(f32[896,64]{0,1:T(8,128)} %param.10) | copy-start | bytes 688132
Sparse Core Ops, SparseCore 0:
  9.8 45.7 all-gather.3
  57.4 63.8 all-gather.5
